TPU v7x, 32 devices: a whole 2x2x4 slice. The times are simulated.
32 devices in a mesh: outer: 8 (over z, core), inner: 4 (over y, x).
Axes of the slice: x: 2, y: 2, z: 4, core: 2. Of those that a mesh axis runs over, the one named last changes fastest.
Arguments:
- queries: bfloat16 [12288, 1536], P(('outer', 'inner')), may hold values from -6 to 6
- key_vectors: bfloat16 [12288, 1536], P(('outer', 'inner')), may hold values from -6 to 6
- value_vectors: bfloat16 [12288, 1536], P(('outer', 'inner')), may hold values from -6 to 6
- write_gate: float32 [12, 12288], P(None, ('outer', 'inner')), may hold values from 0.05 to 1
- ridge_term: float32 [12], replicated, may hold values from 0.25 to 4
- segment_ids: int32 [12288], P(('outer', 'inner')), may hold values from 0 to 15, never falling along the last dimension, each value on 1 to 1536 neighbouring positions
Outputs:
- mixed_heads: bfloat16 [12288, 1536], P(('outer', 'inner'))
Inputs may be any that keep to these rules, and one draw needn't show every extreme that they name: `segment_ids`: segment ids never fall along the tokens; each of the 16 documents spans 1 to 1536 tokens, one exactly 1536.
All inputs are finite; a program needn't handle non-finite values.
Results may differ from a plain program's by a relative error of at most 0.001.
Values sent between devices are 32-bit elements; how exact they have to be, the bound alone decides.
A program may use at most 64 MiB of HBM per device.

v0:
```python
import jax
import jax.numpy as jnp
from jax import lax
from jax.sharding import PartitionSpec as P

STRETCH = 128
ITERS = 4


highest = lax.Precision.HIGHEST


def shifted(block, axis, distance):
    devices = range(lax.axis_size(axis))
    route = [(i - distance, i) for i in devices if i - distance in devices]
    return lax.ppermute(block, axis, route)


def normed_heads(raw, heads):
    rows = raw.shape[0]
    values = raw.astype(jnp.float32).reshape(rows, heads, -1).transpose(1, 0, 2)
    return values * lax.rsqrt(jnp.sum(values * values, axis=-1, keepdims=True) + 1e-06)


def block_step(carry, block, ridge_term):
    gram, memory, previous = carry
    query_raw, key_raw, value_raw, gate_rows, seg_rows = block
    heads = ridge_term.shape[0]
    query_rows = normed_heads(query_raw, heads)
    key_rows = normed_heads(key_raw, heads)
    value_rows = (
        value_raw.astype(jnp.float32).reshape(value_raw.shape[0], heads, -1).transpose(1, 0, 2)
    )
    length = seg_rows.shape[0]
    keep = (seg_rows == previous).astype(jnp.float32)[None, :, None]
    order = jnp.arange(length)
    causal = (seg_rows[:, None] == seg_rows[None, :]) & (order[None, :] <= order[:, None])
    weights = causal.astype(jnp.float32)[None] * gate_rows[:, None, :]
    solved = jnp.zeros_like(query_rows)
    residual = query_rows
    direction = query_rows
    resid_sq = jnp.sum(residual * residual, axis=-1, keepdims=True)
    for sweep in range(ITERS):
        carried = jnp.einsum("hte,hed->htd", direction, gram, precision=highest) * keep
        apply_scores = jnp.einsum("htd,hsd->hts", direction, key_rows, precision=highest) * weights
        inside = jnp.einsum("hts,hsd->htd", apply_scores, key_rows, precision=highest)
        image = carried + inside + ridge_term[:, None, None] * direction
        step_size = resid_sq / jnp.sum(direction * image, axis=-1, keepdims=True)
        solved = solved + step_size * direction
        residual = residual - step_size * image
        fresh_sq = jnp.sum(residual * residual, axis=-1, keepdims=True)
        direction = residual + fresh_sq / resid_sq * direction
        resid_sq = fresh_sq
    carried_out = jnp.einsum("htk,hvk->htv", solved, memory, precision=highest) * keep
    scores = jnp.einsum("htd,hsd->hts", solved, key_rows, precision=highest) * weights
    inside_out = jnp.einsum("hts,hsv->htv", scores, value_rows, precision=highest)
    result = (carried_out + inside_out).transpose(1, 0, 2).reshape(length, -1).astype(jnp.bfloat16)
    last_id = seg_rows[length - 1]
    stay = (last_id == previous).astype(jnp.float32)
    tail = (seg_rows == last_id).astype(jnp.float32)[None, :] * gate_rows
    key_tail = key_rows * tail[:, :, None]
    gram_next = stay * gram + jnp.einsum("hsk,hsl->hkl", key_tail, key_rows, precision=highest)
    memory_next = stay * memory + jnp.einsum(
        "hsv,hsk->hvk", value_rows * tail[:, :, None], key_rows, precision=highest
    )
    return ((gram_next, memory_next, last_id), result)


def combine_states(earlier, later):
    broken = jnp.maximum(later[4], (later[2] != earlier[3]).astype(jnp.float32))
    joined = 1.0 - broken
    return (
        later[0] + joined * earlier[0],
        later[1] + joined * earlier[1],
        earlier[2],
        later[3],
        jnp.maximum(earlier[4], broken),
    )


def body(queries, key_vectors, value_vectors, write_gate, ridge_term, segment_ids):
    tokens_here = queries.shape[0]
    width = queries.shape[1]
    heads = ridge_term.shape[0]
    blocks = tokens_here // STRETCH
    first_id = segment_ids[0]
    last_id = segment_ids[tokens_here - 1]
    key_rows = normed_heads(key_vectors, heads)
    value_rows = (
        value_vectors.astype(jnp.float32).reshape(tokens_here, heads, -1).transpose(1, 0, 2)
    )
    tail = (segment_ids == last_id).astype(jnp.float32)[None, :] * write_gate
    local_gram = jnp.einsum(
        "hsk,hsl->hkl", key_rows * tail[:, :, None], key_rows, precision=highest
    )
    local_memory = jnp.einsum(
        "hsv,hsk->hvk", value_rows * tail[:, :, None], key_rows, precision=highest
    )
    local_flag = (last_id != first_id).astype(jnp.float32)
    local_state = (
        local_gram,
        local_memory,
        first_id.astype(jnp.float32),
        last_id.astype(jnp.float32),
        local_flag,
    )
    running = local_state
    incoming = local_state
    for step in range(4):
        moved = shifted(
            (running[0], running[1], running[2], running[3], running[4]), ("outer", "inner"), 1
        )
        if step < 3:
            running = combine_states(moved, local_state)
        else:
            incoming = moved
    gate_blocks = write_gate.reshape(heads, blocks, STRETCH).transpose(1, 0, 2)
    xs = (
        queries.reshape(blocks, STRETCH, width),
        key_vectors.reshape(blocks, STRETCH, width),
        value_vectors.reshape(blocks, STRETCH, width),
        gate_blocks,
        segment_ids.reshape(blocks, STRETCH),
    )
    init = (incoming[0], incoming[1], incoming[3].astype(jnp.int32))
    final, outputs = lax.scan(lambda carry, block: block_step(carry, block, ridge_term), init, xs)
    return outputs.reshape(tokens_here, width)


def solution(mesh):
    return jax.shard_map(
        body,
        mesh=mesh,
        in_specs=(
            P(("outer", "inner"), None),
            P(("outer", "inner"), None),
            P(("outer", "inner"), None),
            P(None, ("outer", "inner")),
            P(),
            P(("outer", "inner")),
        ),
        out_specs=P(("outer", "inner"), None),
        check_vma=False,
    )
```

profile of v0, /device:TPU:0, one launch (start us, length us, event | category | flops | bytes accessed | tf_op | source)
XLA Modules:
  0.0 267.7 jit_solution(3660517936700325074)
XLA Ops:
  7.1 4.3 %fusion.62 = f32[12,128,128]{2,1,0:T(8,128)S(1)} fusion(bf16[384,12,128]{0,2,1:T(8,128)(2,1)} %bitcast.267, bf16[384,12,128]{0,2,1:T(8,128)(2,1)S(1)} %bitcast.258, f32[12,384]{1,0:T(8,128)S(1)} %get-tuple-element.114, f32[12,384]{1,0:T(8,128)S(1)} %get-tuple-element.113), kind=kOutput, calls=%fused_computation.91 | convolution fusion | flops 908328960 | bytes 3182592 | tf_op jit(solution)/shard_map/hsv,hsk->hvk/dot_general | solution.py:96
  11.4 4.9 %collective-permute-start.5 = (f32[12,128,128]{2,1,0:T(8,128)S(1)}, f32[12,128,128]{2,1,0:T(8,128)S(1)}, u32[]{:S(2)}, u32[]{:S(2)}) collective-permute-start(f32[12,128,128]{2,1,0:T(8,128)S(1)} %fusion.62), channel_id=1, source_target_pairs={{0,1},{1,2},{2,3},{3,4},{4,5},{5,6},{6,7},{7,8},{8,9},{9,10},{10,1... | collective-permute-start | bytes 2359304 | tf_op jit(solution)/shard_map/ppermute | solution.py:16
  16.3 3.2 %fusion.59 = f32[12,128,128]{2,1,0:T(8,128)S(1)} fusion(bf16[384,12,128]{0,2,1:T(8,128)(2,1)S(1)} %bitcast.259, f32[12,384]{1,0:T(8,128)S(1)} %get-tuple-element.114, f32[12,384]{1,0:T(8,128)S(1)} %get-tuple-element.113), kind=kOutput, calls=%fused_computation.87 | convolution fusion | flops 908918784 | bytes 2002944 | tf_op jit(solution)/shard_map/hsk,hsl->hkl/dot_general | solution.py:93
  19.5 3.4 %collective-permute-start.1 = (f32[12,128,128]{2,1,0:T(8,128)S(1)}, f32[12,128,128]{2,1,0:T(8,128)S(1)}, u32[]{:S(2)}, u32[]{:S(2)}) collective-permute-start(f32[12,128,128]{2,1,0:T(8,128)S(1)} %fusion.59), channel_id=1, source_target_pairs={{0,1},{1,2},{2,3},{3,4},{4,5},{5,6},{6,7},{7,8},{8,9},{9,10},{10,1... | collective-permute-start | bytes 2359304 | tf_op jit(solution)/shard_map/ppermute | solution.py:16
  23.6 26.4 %collective-permute-start = (f32[]{:T(128)}, f32[]{:T(128)}, u32[]{:S(2)}, u32[]{:S(2)}) collective-permute-start(f32[]{:T(128)} %convert_element_type.72), channel_id=1, source_target_pairs={{0,1},{1,2},{2,3},{3,4},{4,5},{5,6},{6,7},{7,8},{8,9},{9,10},{10,1... | collective-permute-start | bytes 20 | tf_op jit(solution)/shard_map/ppermute | solution.py:16
  52.5 3.4 %collective-permute-start.6 = (f32[12,128,128]{2,1,0:T(8,128)S(1)}, f32[12,128,128]{2,1,0:T(8,128)S(1)}, u32[]{:S(2)}, u32[]{:S(2)}) collective-permute-start(f32[12,128,128]{2,1,0:T(8,128)S(1)} %multiply_add_fusion.4), channel_id=1, source_target_pairs={{0,1},{1,2},{2,3},{3,4},{4,5},{5,6},{6,7},{7,8},{8,9},{9,10},{10,1... | collective-permute-start | bytes 2359304 | tf_op jit(solution)/shard_map/ppermute | solution.py:16
  56.1 3.5 %collective-permute-start.2 = (f32[12,128,128]{2,1,0:T(8,128)S(1)}, f32[12,128,128]{2,1,0:T(8,128)S(1)}, u32[]{:S(2)}, u32[]{:S(2)}) collective-permute-start(f32[12,128,128]{2,1,0:T(8,128)S(1)} %multiply_add_fusion.7), channel_id=1, source_target_pairs={{0,1},{1,2},{2,3},{3,4},{4,5},{5,6},{6,7},{7,8},{8,9},{9,10},{10,1... | collective-permute-start | bytes 2359304 | tf_op jit(solution)/shard_map/ppermute | solution.py:16
  59.6 14.3 %collective-permute-done.6 = f32[12,128,128]{2,1,0:T(8,128)S(1)} collective-permute-done((f32[12,128,128]{2,1,0:T(8,128)S(1)}, f32[12,128,128]{2,1,0:T(8,128)S(1)}, u32[]{:S(2)}, u32[]{:S(2)}) %collective-permute-start.6) | collective-permute-done | bytes 786464 | tf_op jit(solution)/shard_map/ppermute | solution.py:16
  74.0 4.4 %collective-permute-start.7 = (f32[12,128,128]{2,1,0:T(8,128)S(1)}, f32[12,128,128]{2,1,0:T(8,128)S(1)}, u32[]{:S(2)}, u32[]{:S(2)}) collective-permute-start(f32[12,128,128]{2,1,0:T(8,128)S(1)} %multiply_add_fusion.3), channel_id=1, source_target_pairs={{0,1},{1,2},{2,3},{3,4},{4,5},{5,6},{6,7},{7,8},{8,9},{9,10},{10,1... | collective-permute-start | bytes 2359304 | tf_op jit(solution)/shard_map/ppermute | solution.py:16
  78.4 12.3 %collective-permute-done.2 = f32[12,128,128]{2,1,0:T(8,128)S(1)} collective-permute-done((f32[12,128,128]{2,1,0:T(8,128)S(1)}, f32[12,128,128]{2,1,0:T(8,128)S(1)}, u32[]{:S(2)}, u32[]{:S(2)}) %collective-permute-start.2) | collective-permute-done | bytes 786464 | tf_op jit(solution)/shard_map/ppermute | solution.py:16
  90.9 4.4 %collective-permute-start.3 = (f32[12,128,128]{2,1,0:T(8,128)S(1)}, f32[12,128,128]{2,1,0:T(8,128)S(1)}, u32[]{:S(2)}, u32[]{:S(2)}) collective-permute-start(f32[12,128,128]{2,1,0:T(8,128)S(1)} %multiply_add_fusion.6), channel_id=1, source_target_pairs={{0,1},{1,2},{2,3},{3,4},{4,5},{5,6},{6,7},{7,8},{8,9},{9,10},{10,1... | collective-permute-start | bytes 2359304 | tf_op jit(solution)/shard_map/ppermute | solution.py:16
  95.3 12.3 %collective-permute-done.7 = f32[12,128,128]{2,1,0:T(8,128)S(1)} collective-permute-done((f32[12,128,128]{2,1,0:T(8,128)S(1)}, f32[12,128,128]{2,1,0:T(8,128)S(1)}, u32[]{:S(2)}, u32[]{:S(2)}) %collective-permute-start.7) | collective-permute-done | bytes 786464 | tf_op jit(solution)/shard_map/ppermute | solution.py:16
  107.7 4.4 %collective-permute-start.8 = (f32[12,128,128]{2,1,0:T(8,128)S(1)}, f32[12,128,128]{2,1,0:T(8,128)S(1)}, u32[]{:S(2)}, u32[]{:S(2)}) collective-permute-start(f32[12,128,128]{2,1,0:T(8,128)S(1)} %multiply_add_fusion.2), channel_id=1, source_target_pairs={{0,1},{1,2},{2,3},{3,4},{4,5},{5,6},{6,7},{7,8},{8,9},{9,10},{10,1... | collective-permute-start | bytes 2359304 | tf_op jit(solution)/shard_map/ppermute | solution.py:16
  112.2 12.3 %collective-permute-done.3 = f32[12,128,128]{2,1,0:T(8,128)S(1)} collective-permute-done((f32[12,128,128]{2,1,0:T(8,128)S(1)}, f32[12,128,128]{2,1,0:T(8,128)S(1)}, u32[]{:S(2)}, u32[]{:S(2)}) %collective-permute-start.3) | collective-permute-done | bytes 786464 | tf_op jit(solution)/shard_map/ppermute | solution.py:16
  124.6 4.4 %collective-permute-start.4 = (f32[12,128,128]{2,1,0:T(8,128)S(1)}, f32[12,128,128]{2,1,0:T(8,128)S(1)}, u32[]{:S(2)}, u32[]{:S(2)}) collective-permute-start(f32[12,128,128]{2,1,0:T(8,128)S(1)} %multiply_add_fusion.5), channel_id=1, source_target_pairs={{0,1},{1,2},{2,3},{3,4},{4,5},{5,6},{6,7},{7,8},{8,9},{9,10},{10,1... | collective-permute-start | bytes 2359304 | tf_op jit(solution)/shard_map/ppermute | solution.py:16
  129.7 11.6 %collective-permute-done.8 = f32[12,128,128]{2,1,0:T(8,128)S(1)} collective-permute-done((f32[12,128,128]{2,1,0:T(8,128)S(1)}, f32[12,128,128]{2,1,0:T(8,128)S(1)}, u32[]{:S(2)}, u32[]{:S(2)}) %collective-permute-start.8) | collective-permute-done | bytes 786464 | tf_op jit(solution)/shard_map/ppermute | solution.py:16
  141.3 14.8 %collective-permute-done.4 = f32[12,128,128]{2,1,0:T(8,128)S(1)} collective-permute-done((f32[12,128,128]{2,1,0:T(8,128)S(1)}, f32[12,128,128]{2,1,0:T(8,128)S(1)}, u32[]{:S(2)}, u32[]{:S(2)}) %collective-permute-start.4) | collective-permute-done | bytes 786464 | tf_op jit(solution)/shard_map/ppermute | solution.py:16
  156.1 111.5 %while.16 = (s32[]{:T(128)}, f32[12,128,128]{2,1,0:T(8,128)S(1)}, f32[12,128,128]{2,1,0:T(8,128)S(1)}, s32[]{:T(128)}, bf16[3,128,1536]{2,1,0:T(8,128)(2,1)}, /*...) while((s32[]{:T(128)}, f32[12,128,128]{2,1,0:T(8,128)S(1)}, ...), condition=%wide.region_12.13_spmd, body=%wide.region_1.12_spmd.sunk | while | flops 5157683712 | bytes 65131716 | solution.py:126
  181.5 2.3 multiply_multiply_fusion.14
  185.0 2.1 fusion.172
  218.7 2.3 multiply_multiply_fusion.14
  222.1 2.1 fusion.172
  255.8 2.3 multiply_multiply_fusion.14
  259.3 2.1 fusion.172
  (193 shorter events, 101.0 us)
Async XLA Ops:
  11.4 41.0 %collective-permute-start.5 = (f32[12,128,128]{2,1,0:T(8,128)S(1)}, f32[12,128,128]{2,1,0:T(8,128)S(1)}, u32[]{:S(2)}, u32[]{:S(2)}) collective-permute-start(f32[12,128,128]{2,1,0:T(8,128)S(1)} %fusion.62), channel_id=1, source_target_pairs={{0,1},{1,2},{2,3},{3,4},{4,5},{5,6},{6,7},{7,8},{8,9},{9,10},{10,1... | collective-permute-start | bytes 2359304 | tf_op jit(solution)/shard_map/ppermute | solution.py:16
  19.5 36.5 %collective-permute-start.1 = (f32[12,128,128]{2,1,0:T(8,128)S(1)}, f32[12,128,128]{2,1,0:T(8,128)S(1)}, u32[]{:S(2)}, u32[]{:S(2)}) collective-permute-start(f32[12,128,128]{2,1,0:T(8,128)S(1)} %fusion.59), channel_id=1, source_target_pairs={{0,1},{1,2},{2,3},{3,4},{4,5},{5,6},{6,7},{7,8},{8,9},{9,10},{10,1... | collective-permute-start | bytes 2359304 | tf_op jit(solution)/shard_map/ppermute | solution.py:16
  23.6 28.1 %collective-permute-start = (f32[]{:T(128)}, f32[]{:T(128)}, u32[]{:S(2)}, u32[]{:S(2)}) collective-permute-start(f32[]{:T(128)} %convert_element_type.72), channel_id=1, source_target_pairs={{0,1},{1,2},{2,3},{3,4},{4,5},{5,6},{6,7},{7,8},{8,9},{9,10},{10,1... | collective-permute-start | bytes 20 | tf_op jit(solution)/shard_map/ppermute | solution.py:16
  52.5 21.4 %collective-permute-start.6 = (f32[12,128,128]{2,1,0:T(8,128)S(1)}, f32[12,128,128]{2,1,0:T(8,128)S(1)}, u32[]{:S(2)}, u32[]{:S(2)}) collective-permute-start(f32[12,128,128]{2,1,0:T(8,128)S(1)} %multiply_add_fusion.4), channel_id=1, source_target_pairs={{0,1},{1,2},{2,3},{3,4},{4,5},{5,6},{6,7},{7,8},{8,9},{9,10},{10,1... | collective-permute-start | bytes 2359304 | tf_op jit(solution)/shard_map/ppermute | solution.py:16
  56.1 34.7 %collective-permute-start.2 = (f32[12,128,128]{2,1,0:T(8,128)S(1)}, f32[12,128,128]{2,1,0:T(8,128)S(1)}, u32[]{:S(2)}, u32[]{:S(2)}) collective-permute-start(f32[12,128,128]{2,1,0:T(8,128)S(1)} %multiply_add_fusion.7), channel_id=1, source_target_pairs={{0,1},{1,2},{2,3},{3,4},{4,5},{5,6},{6,7},{7,8},{8,9},{9,10},{10,1... | collective-permute-start | bytes 2359304 | tf_op jit(solution)/shard_map/ppermute | solution.py:16
  74.0 33.6 %collective-permute-start.7 = (f32[12,128,128]{2,1,0:T(8,128)S(1)}, f32[12,128,128]{2,1,0:T(8,128)S(1)}, u32[]{:S(2)}, u32[]{:S(2)}) collective-permute-start(f32[12,128,128]{2,1,0:T(8,128)S(1)} %multiply_add_fusion.3), channel_id=1, source_target_pairs={{0,1},{1,2},{2,3},{3,4},{4,5},{5,6},{6,7},{7,8},{8,9},{9,10},{10,1... | collective-permute-start | bytes 2359304 | tf_op jit(solution)/shard_map/ppermute | solution.py:16
  90.9 33.6 %collective-permute-start.3 = (f32[12,128,128]{2,1,0:T(8,128)S(1)}, f32[12,128,128]{2,1,0:T(8,128)S(1)}, u32[]{:S(2)}, u32[]{:S(2)}) collective-permute-start(f32[12,128,128]{2,1,0:T(8,128)S(1)} %multiply_add_fusion.6), channel_id=1, source_target_pairs={{0,1},{1,2},{2,3},{3,4},{4,5},{5,6},{6,7},{7,8},{8,9},{9,10},{10,1... | collective-permute-start | bytes 2359304 | tf_op jit(solution)/shard_map/ppermute | solution.py:16
  107.7 21.3 %copy-start.8 = (f32[12,384]{1,0:T(8,128)S(1)}, f32[12,384]{1,0:T(8,128)}, u32[]{:S(2)}) copy-start(f32[12,384]{1,0:T(8,128)} %param.11) | copy-start | bytes 55300
  107.7 48.4 %copy-start.3 = (f32[12]{0:T(128)S(1)}, f32[12]{0:T(128)}, u32[]{:S(2)}) copy-start(f32[12]{0:T(128)} %param.12) | copy-start | bytes 148
  107.7 33.6 %collective-permute-start.8 = (f32[12,128,128]{2,1,0:T(8,128)S(1)}, f32[12,128,128]{2,1,0:T(8,128)S(1)}, u32[]{:S(2)}, u32[]{:S(2)}) collective-permute-start(f32[12,128,128]{2,1,0:T(8,128)S(1)} %multiply_add_fusion.2), channel_id=1, source_target_pairs={{0,1},{1,2},{2,3},{3,4},{4,5},{5,6},{6,7},{7,8},{8,9},{9,10},{10,1... | collective-permute-start | bytes 2359304 | tf_op jit(solution)/shard_map/ppermute | solution.py:16
  124.6 31.5 %collective-permute-start.4 = (f32[12,128,128]{2,1,0:T(8,128)S(1)}, f32[12,128,128]{2,1,0:T(8,128)S(1)}, u32[]{:S(2)}, u32[]{:S(2)}) collective-permute-start(f32[12,128,128]{2,1,0:T(8,128)S(1)} %multiply_add_fusion.5), channel_id=1, source_target_pairs={{0,1},{1,2},{2,3},{3,4},{4,5},{5,6},{6,7},{7,8},{8,9},{9,10},{10,1... | collective-permute-start | bytes 2359304 | tf_op jit(solution)/shard_map/ppermute | solution.py:16
  156.1 4.5 %copy-start.5 = (f32[3,12,128]{2,0,1:T(4,128)}, f32[3,12,128]{2,0,1:T(4,128)S(1)}, u32[]{:S(2)}) copy-start(f32[3,12,128]{2,0,1:T(4,128)S(1)} %get-tuple-element.243) | copy-start | bytes 55300 | tf_op jit(solution)/shard_map/while
  156.8 21.1 %copy-start.1 = (f32[128]{0:T(128)}, f32[128]{0:T(128)S(1)}, u32[]{:S(2)}) copy-start(f32[128]{0:T(128)S(1)} %get-tuple-element.202) | copy-start | bytes 1540 | tf_op jit(solution)/shard_map/while
  181.5 2.4 copy-start.2
  190.6 2.0 copy-start.4
  190.6 2.0 copy-start.6
  193.3 4.6 %copy-start.5 = (f32[3,12,128]{2,0,1:T(4,128)}, f32[3,12,128]{2,0,1:T(4,128)S(1)}, u32[]{:S(2)}) copy-start(f32[3,12,128]{2,0,1:T(4,128)S(1)} %get-tuple-element.243) | copy-start | bytes 55300 | tf_op jit(solution)/shard_map/while
  194.0 21.1 %copy-start.1 = (f32[128]{0:T(128)}, f32[128]{0:T(128)S(1)}, u32[]{:S(2)}) copy-start(f32[128]{0:T(128)S(1)} %get-tuple-element.202) | copy-start | bytes 1540 | tf_op jit(solution)/shard_map/while
  218.7 2.4 copy-start.2
  227.8 2.0 copy-start.4
  230.4 4.6 %copy-start.5 = (f32[3,12,128]{2,0,1:T(4,128)}, f32[3,12,128]{2,0,1:T(4,128)S(1)}, u32[]{:S(2)}) copy-start(f32[3,12,128]{2,0,1:T(4,128)S(1)} %get-tuple-element.243) | copy-start | bytes 55300 | tf_op jit(solution)/shard_map/while
  231.1 21.1 %copy-start.1 = (f32[128]{0:T(128)}, f32[128]{0:T(128)S(1)}, u32[]{:S(2)}) copy-start(f32[128]{0:T(128)S(1)} %get-tuple-element.202) | copy-start | bytes 1540 | tf_op jit(solution)/shard_map/while
  255.8 2.4 copy-start.2
  264.9 2.0 copy-start.4
  (4 other events, 6.7 us)
where the time goes:
time: 272 us; the launch traced here: 268 us
  matrix products  91.4 us (34%)
  waiting for transfers between devices  77.6 us (29%)
  starting transfers between devices  59.4 us (22%)
  local copies, waits for them, and re-layouts  19 us (7%)
  other arithmetic  11.4 us (4%)
  loops' own time  4.8 us (2%)
  between operations  4.15 us (2%)
    ppermute x9, waiting for transfers between devices, shifted(): return lax.ppermute(block, axis, route)  77.6 us
    ppermute x9, starting transfers between devices, shifted(): return lax.ppermute(block, axis, route)  59.4 us
    dot_general x12, matrix products, block_step(): jnp.einsum('hts,hsd->htd', apply_scores, key_rows, precision=highest)  21.6 us
    dot_general x12, matrix products, block_step(): jnp.einsum('htd,hsd->hts', direction, key_rows, precision=highest) * weights  17.5 us
    dot_general x12, matrix products, block_step(): jnp.einsum('hte,hed->htd', direction, gram, precision=highest) * keep  17.1 us
    dynamic_slice x21, local copies, waits for them, and re-layouts, body(): lax.scan(lambda carry, block: block_step(carry, block, ridge_term), init,...  8.62 us
    dot_general x3, matrix products, block_step(): jnp.einsum('htd,hsd->hts', solved, key_rows, precision=highest) * weights  7.03 us
    dot_general x3, matrix products, block_step(): jnp.einsum('hts,hsv->htv', scores, value_rows, precision=highest)  6.28 us
  transfers between devices with their start and end apart: 9, of which 6 were waited for; matrix products, arithmetic and copies ran while one was open for 1% of the time, Pallas kernels for 0%

commit v1 on v0

v1 whole, which is shorter than its diff:
```python
import functools

import jax
import jax.numpy as jnp
from jax import lax
from jax.experimental import pallas as pl
from jax.experimental.pallas import tpu as pltpu
from jax.sharding import PartitionSpec as P

STRETCH = 128
ITERS = 4
LAG = 2
MESH = pl.DeviceIdType.MESH
F32 = jnp.float32
BF16 = jnp.bfloat16


def split(x):
    hi = x.astype(BF16)
    return hi, (x - hi.astype(F32)).astype(BF16)


def mm(a, b):
    return jnp.dot(a, b, preferred_element_type=F32)


def same(a, b):
    return (a == b).astype(F32)


def kernel(
    sizes, q_ref, k_ref, v_ref, gate_ref, ridge_ref, seg_ref, o_ref,
    causal, keep, kt_buf, gram_row, memory_row, part,
    local, got1, pair, got2, suffix, got3, id_out, id_in,
    send1, recv1, send2, recv2, send3, recv3, id_send, id_recv,
):
    outer, inner = sizes
    devices = outer * inner
    heads = gate_ref.shape[0]
    blocks = q_ref.shape[0] // STRETCH
    me = lax.axis_index("outer") * inner + lax.axis_index("inner")
    spot = me % 4
    odd_i, top_i = spot % 2, spot // 2

    def place(index):
        return (index // inner, index % inner)

    across1 = place(me + 1 - 2 * odd_i)
    across2 = place(me + 2 - 4 * top_i)
    after = place((me + 4) % devices)
    before = place((me + devices - 4) % devices)

    barrier = pltpu.get_barrier_semaphore()
    for target in (across1, across2, before):
        pl.semaphore_signal(barrier, inc=1, device_id=target, device_id_type=MESH)
    pl.semaphore_wait(barrier, 3)

    def exchange(src, dst, sender, receiver, target):
        return pltpu.make_async_remote_copy(
            src_ref=src, dst_ref=dst, send_sem=sender, recv_sem=receiver,
            device_id=target, device_id_type=MESH,
        )

    def phase1(h):
        return exchange(local.at[h], got1.at[h], send1.at[h], recv1.at[h], across1)

    def phase2(h):
        return exchange(pair.at[h], got2.at[h], send2.at[h], recv2.at[h], across2)

    def phase3(h):
        return exchange(suffix.at[h], got3.at[h], send3.at[h], recv3.at[h], after)

    def id_phase(p):
        target = (across1, across2, after)[p]
        return exchange(id_out.at[p], id_in.at[p], id_send.at[p], id_recv.at[p], target)

    seg = seg_ref[...].astype(F32)
    first = seg[0:1, 0:1]
    rows = [seg[b:b + 1, :] for b in range(blocks)]
    last = [seg[b:b + 1, STRETCH - 1:STRETCH] for b in range(blocks)]

    id_out[0] = jnp.broadcast_to(last[-1], (8, 128))
    id_phase(0).start()

    odd, top = odd_i.astype(F32), top_i.astype(F32)
    for b in range(blocks):
        grid_rows = jnp.broadcast_to(rows[b], (STRETCH, STRETCH))
        grid_cols = grid_rows.T
        down = lax.broadcasted_iota(jnp.int32, (STRETCH, STRETCH), 0)
        over = lax.broadcasted_iota(jnp.int32, (STRETCH, STRETCH), 1)
        causal[b] = jnp.where(over <= down, same(grid_rows, grid_cols), 0.0)
        keep[b] = same(grid_cols, first if b == 0 else last[b - 1]).astype(BF16)

    tails = [same(rows[b], last[b]) for b in range(blocks)]

    def columns(h):
        return pl.ds(pl.multiple_of(h * 128, 128), 128)

    def span(b):
        return slice(b * STRETCH, (b + 1) * STRETCH)

    def gather_local(h, carry):
        total = jnp.zeros((256, 128), F32)
        for b in range(blocks):
            keys = k_ref[span(b), columns(h)]
            values = v_ref[span(b), columns(h)]
            wide = keys.astype(F32).T
            kt_buf[h, b] = wide.astype(BF16)
            scale = lax.rsqrt(jnp.sum(wide * wide, axis=0, keepdims=True) + 1e-06)
            w1 = memory_row[h, b] * scale
            w2 = w1 * scale
            memory_row[h, b] = w1
            gram_row[h, b] = w2
            ghi, glo = split(wide * (w2 * tails[b]))
            mhi, mlo = split(wide * (w1 * tails[b]))
            gram = mm(jnp.concatenate([ghi, glo], 1), jnp.concatenate([keys, keys], 0))
            memory = mm(jnp.concatenate([mhi, mlo], 1), jnp.concatenate([values, values], 0))
            both = jnp.concatenate([gram, memory], 0)
            if b < blocks - 1:
                part[h, b] = both
            total = total + same(last[b], last[-1]) * both
        local[h] = total
        phase1(h).start()
        return carry

    for h in range(heads):
        for b in range(blocks):
            memory_row[h, b] = gate_ref[h:h + 1, span(b)]
    lax.fori_loop(0, heads, gather_local, 0)

    id_phase(0).wait_recv()
    other_last = id_in[0][0:1, 0:1]
    equal = same(last[-1], other_last)
    pair_local = odd + (1.0 - odd) * equal
    pair_got = (1.0 - odd) + odd * equal
    pair_id = odd * last[-1] + (1.0 - odd) * other_last
    id_out[1] = jnp.broadcast_to(pair_id, (8, 128))
    id_phase(1).start()
    id_phase(1).wait_recv()
    far_id = id_in[1][0:1, 0:1]
    base = top + (1.0 - top) * same(pair_id, far_id)
    suffix_local = base * (odd + (1.0 - odd) * pair_local)
    suffix_got = base * (1.0 - odd) * pair_got
    id_out[2] = jnp.broadcast_to(top * pair_id + (1.0 - top) * far_id, (8, 128))
    id_phase(2).start()
    id_phase(2).wait_recv()
    in1 = odd * same(other_last, first)
    in2 = top * same(far_id, first)
    in3 = same(id_in[2][0:1, 0:1], first)

    def solve(h):
        ridge = ridge_ref[h]
        state = in1 * got1[h] + in2 * got2[h] + in3 * got3[h]
        keys, lifts, mems, kts, weights, masks = [], [], [], [], [], []
        xs, rs, ds, sqs = [], [], [], []
        for b in range(blocks):
            if b > 0:
                previous = first if b == 1 else last[b - 2]
                state = part[h, b - 1] + same(last[b - 1], previous) * state
            hi, lo = split(state)
            k = k_ref[span(b), columns(h)]
            v = v_ref[span(b), columns(h)]
            lifts.append(jnp.concatenate([k, k, hi[:128], hi[:128], lo[:128]], 0))
            mems.append(jnp.concatenate([v, v, hi[128:], hi[128:], lo[128:]], 0))
            kt = kt_buf[h, b]
            kts.append(jnp.concatenate([kt, kt], 0))
            weights.append(causal[b] * gram_row[h, b])
            q = q_ref[span(b), columns(h)].astype(F32)
            q = q * lax.rsqrt(jnp.sum(q * q, axis=-1, keepdims=True) + 1e-06)
            xs.append(jnp.zeros_like(q))
            rs.append(q)
            ds.append(q)
            sqs.append(jnp.sum(q * q, axis=-1, keepdims=True))

        def apply(b, d, weight, lift):
            hi, lo = split(d)
            scores = mm(jnp.concatenate([hi, lo], 1), kts[b]) * weight
            shi, slo = split(scores)
            mask = keep[b]
            khi, klo = hi * mask, lo * mask
            return mm(jnp.concatenate([shi, slo, khi, klo, khi], 1), lift)

        for sweep in range(ITERS):
            for b in range(blocks):
                d = ds[b]
                image = apply(b, d, weights[b], lifts[b]) + ridge * d
                size = sqs[b] / jnp.sum(d * image, axis=-1, keepdims=True)
                xs[b] = xs[b] + size * d
                if sweep < ITERS - 1:
                    rs[b] = rs[b] - size * image
                    fresh = jnp.sum(rs[b] * rs[b], axis=-1, keepdims=True)
                    ds[b] = rs[b] + fresh / sqs[b] * d
                    sqs[b] = fresh
        for b in range(blocks):
            out = apply(b, xs[b], causal[b] * memory_row[h, b], mems[b])
            o_ref[span(b), columns(h)] = out.astype(BF16)

    def stage(t, carry):
        @pl.when(t < heads)
        def _():
            phase1(t).wait_recv()
            pair[t] = pair_local * local[t] + pair_got * got1[t]
            phase2(t).start()

        @pl.when(t >= LAG)
        def _():
            phase3(t - LAG).wait_recv()
            solve(t - LAG)

        @pl.when(t < heads)
        def _():
            phase2(t).wait_recv()
            suffix[t] = (
                (1.0 - top) * got2[t] + suffix_local * local[t] + suffix_got * got1[t]
            )
            phase3(t).start()

        return carry

    lax.fori_loop(0, heads + LAG, stage, 0)

    def drain(h, carry):
        phase1(h).wait_send()
        phase2(h).wait_send()
        phase3(h).wait_send()
        return carry

    lax.fori_loop(0, heads, drain, 0)
    for p in range(3):
        id_phase(p).wait_send()


def body(sizes, queries, key_vectors, value_vectors, write_gate, ridge_term, segment_ids):
    tokens, width = queries.shape
    heads = ridge_term.shape[0]
    blocks = tokens // STRETCH
    vmem = pl.BlockSpec(memory_space=pltpu.VMEM)
    smem = pl.BlockSpec(memory_space=pltpu.SMEM)
    state = pltpu.VMEM((heads, 256, 128), F32)
    return pl.pallas_call(
        functools.partial(kernel, sizes),
        out_shape=jax.ShapeDtypeStruct((tokens, width), BF16),
        in_specs=[vmem, vmem, vmem, vmem, smem, vmem],
        out_specs=vmem,
        scratch_shapes=[
            pltpu.VMEM((blocks, STRETCH, STRETCH), F32),
            pltpu.VMEM((blocks, STRETCH, STRETCH), BF16),
            pltpu.VMEM((heads, blocks, 128, STRETCH), BF16),
            pltpu.VMEM((heads, blocks, 1, STRETCH), F32),
            pltpu.VMEM((heads, blocks, 1, STRETCH), F32),
            pltpu.VMEM((heads, blocks - 1, 256, 128), F32),
            state, state, state, state, state, state,
            pltpu.VMEM((3, 8, 128), F32),
            pltpu.VMEM((3, 8, 128), F32),
        ] + [pltpu.SemaphoreType.DMA((heads,))] * 6 + [pltpu.SemaphoreType.DMA((3,))] * 2,
        compiler_params=pltpu.CompilerParams(
            collective_id=0, has_side_effects=True, vmem_limit_bytes=50 * 1024 * 1024
        ),
        cost_estimate=pl.CostEstimate(
            flops=6_000_000_000, bytes_accessed=6_000_000, transcendentals=0
        ),
    )(
        queries, key_vectors, value_vectors, write_gate, ridge_term,
        segment_ids.reshape(blocks, STRETCH),
    )


def solution(mesh):
    sizes = (mesh.shape["outer"], mesh.shape["inner"])
    return jax.shard_map(
        functools.partial(body, sizes),
        mesh=mesh,
        in_specs=(
            P(("outer", "inner"), None),
            P(("outer", "inner"), None),
            P(("outer", "inner"), None),
            P(None, ("outer", "inner")),
            P(),
            P(("outer", "inner")),
        ),
        out_specs=P(("outer", "inner"), None),
        check_vma=False,
    )
```

time: 272 us -> 85.1 us (0.31); the launches traced: 268 us -> 84.8 us
  matrix products: 91.4 us -> 0 us
  Pallas kernels: 0 us -> 79.2 us
  waiting for transfers between devices: 77.6 us -> 0 us
  starting transfers between devices: 59.4 us -> 0 us
  local copies, waits for them, and re-layouts: 19 us -> 5.63 us
  other arithmetic: 11.4 us -> 0 us
  loops' own time: 4.8 us -> 0 us
  between operations: 4.15 us -> 0.01 us
    dot_general x53 -> x0, matrix products: 91.4 us -> none  [the longest x12 21.6 us: block_step(): jnp.einsum('hts,hsd->htd', apply_scores, key_rows, precision=highest)]
    pallas_call x0 -> x1, Pallas kernels: none -> 79.2 us  [body(): pl.pallas_call(functools.partial(kernel, sizes), out_shape=jax.ShapeDtype...]
    ppermute x9 -> x0, waiting for transfers between devices: 77.6 us -> none  [shifted(): return lax.ppermute(block, axis, route)]
    ppermute x9 -> x0, starting transfers between devices: 59.4 us -> none  [shifted(): return lax.ppermute(block, axis, route)]
    dynamic_slice x21 -> x0, local copies, waits for them, and re-layouts: 8.62 us -> none  [body(): lax.scan(lambda carry, block: block_step(carry, block, ridge_term), init,...]
    another operation x1 -> x0, loops' own time: 4.8 us -> none  [body(): lax.scan(lambda carry, block: block_step(carry, block, ridge_term), init,...]
    convert_element_type x7 -> x0, other arithmetic: 3.65 us -> none  [the longest x3 2.09 us: block_step(): keep = (seg_rows == previous).astype(jnp.float32)[None, :, None]]
    slice x4 -> x0, local copies, waits for them, and re-layouts: 3.3 us -> none  [the longest x3 1.93 us: block_step(): last_id = seg_rows[length - 1]]
  transfers between devices with their start and end apart: 9 -> 0, of which waited for: 6 -> 0; matrix products, arithmetic and copies ran while one was open for 1% -> 0% of each run, Pallas kernels for 0% -> 0%
where the time goes in v1:
time: 85.1 us; the launch traced here: 84.8 us
  Pallas kernels  79.2 us (93%)
  local copies, waits for them, and re-layouts  5.63 us (7%)
    pallas_call x1, Pallas kernels, body(): pl.pallas_call(functools.partial(kernel, sizes), out_shape=jax.ShapeDtype...  79.2 us
    unnamed x11, local copies, waits for them, and re-layouts  5.63 us

profile of v1, /device:TPU:0, one launch (start us, length us, event | category | flops | bytes accessed | tf_op | source)
XLA Modules:
  0.0 84.8 jit_solution(5571801925990359577)
XLA Ops:
  0.0 0.0 copy-start
  0.0 1.3 %copy-done = bf16[384,1536]{1,0:T(8,128)(2,1)S(1)} copy-done((bf16[384,1536]{1,0:T(8,128)(2,1)S(1)}, bf16[384,1536]{1,0:T(8,128)(2,1)}, u32[]{:S(2)}) %copy-start) | copy-done | bytes 1179672
  1.3 0.0 copy-start.1
  1.3 1.3 %copy-done.1 = bf16[384,1536]{1,0:T(8,128)(2,1)S(1)} copy-done((bf16[384,1536]{1,0:T(8,128)(2,1)S(1)}, bf16[384,1536]{1,0:T(8,128)(2,1)}, u32[]{:S(2)}) %copy-start.1) | copy-done | bytes 1179672
  2.5 0.0 copy-start.2
  2.5 0.7 copy-done.2
  3.3 0.0 copy-start.3
  3.3 0.7 copy-done.3
  4.0 0.0 copy-start.4
  4.0 0.7 copy-done.4
  4.6 79.2 %shard_map.64 = bf16[384,1536]{1,0:T(8,128)(2,1)S(1)} custom-call(bf16[384,1536]{1,0:T(8,128)(2,1)S(1)} %copy-done, bf16[384,1536]{1,0:T(8,128)(2,1)S(1)} %copy-done.1, bf16[384,1536]{1,0:T(8,128)(2,1)} %v_ref.1, f32[12,384]{1,0:T(8,128)S(1)} %copy-done.2, f32[12]{0:T(128)S(1)} %copy-done.4, s32[3,128]{1,0:T(4,128)S(1)} %bitcast.1), custom_call_target="tpu_custom_call" | custom-call | flops 6000000000 | bytes 6000000 | tf_op jit(solution)/shard_map/pallas_call | solution.py:240
  83.8 1.0 %copy.8 = bf16[384,1536]{1,0:T(8,128)(2,1)} copy(bf16[384,1536]{1,0:T(8,128)(2,1)S(1)} %shard_map.64) | data formatting | bytes 2359296
Async XLA Ops:
  0.0 1.3 %copy-start = (bf16[384,1536]{1,0:T(8,128)(2,1)S(1)}, bf16[384,1536]{1,0:T(8,128)(2,1)}, u32[]{:S(2)}) copy-start(bf16[384,1536]{1,0:T(8,128)(2,1)} %q_ref.1) | copy-start | bytes 3538948
  1.3 1.3 %copy-start.1 = (bf16[384,1536]{1,0:T(8,128)(2,1)S(1)}, bf16[384,1536]{1,0:T(8,128)(2,1)}, u32[]{:S(2)}) copy-start(bf16[384,1536]{1,0:T(8,128)(2,1)} %k_ref.1) | copy-start | bytes 3538948
  2.5 0.7 copy-start.2
  3.3 0.7 copy-start.3
  4.0 0.7 copy-start.4
